TPU v7x, 256 devices: a whole 4x4x8 slice. The times are simulated.
256 devices in a mesh: tok: 16 (over x_lo, y, core), voc: 16 (over x_hi, z).
Axes of the slice: x: 4 (x_hi: 2, x_lo: 2; x = x_hi * 2 + x_lo), y: 4, z: 8, core: 2. Of those that a mesh axis runs over, the one named last changes fastest.
Arguments:
- resid: bfloat16 [512, 3584], P('tok'), may hold values from -50 to 50
- norm_gain: float32 [3584], replicated, may hold values from 0.5 to 1.5
- unembed: bfloat16 [3584, 196608], P(None, ('tok', 'voc')), may hold values from -0.7349684 to 0.7349684
- targets: int32 [512], replicated, may hold values from 0 to 196607
- feat_ids: int32 [512, 64], P('tok'), may hold values from 0 to 16383, all different within a row
- feat_acts: float32 [512, 64], P('tok'), may hold values from 0.5 to 4
- decoder: bfloat16 [3584, 16384], P('voc'), may hold values from -1.796875 to 1.796875
Outputs:
- attribution: float32 [512, 64], P('tok')
All inputs are finite; a program needn't handle non-finite values.
Results may differ from a plain program's by a relative error of at most 0.0029.
Values may be sent and summed in bfloat16 or wider, within the bound.
A program may use at most 128 MiB of HBM per device.

v0:
```python
import jax
import jax.numpy as jnp
from jax import lax
from jax.sharding import PartitionSpec as P

EPSILON = 1e-06


def project_columns(picked, grads, tok_rows, active):
    spread = jnp.repeat(jnp.transpose(grads), active, axis=1)
    return jnp.sum(picked * spread, axis=0).reshape(tok_rows, active)


def on_device(resid, norm_gain, unembed, targets, feat_ids, feat_acts, decoder):
    tok_rows, model_width = resid.shape
    active = feat_ids.shape[1]
    voc_cols = unembed.shape[1]
    tok_count = lax.axis_size("tok")
    voc_count = lax.axis_size("voc")
    slab_width = decoder.shape[0]
    hidden = resid.astype(jnp.float32)
    row_rms = jnp.sqrt(jnp.mean(hidden * hidden, axis=1) + EPSILON)
    normed = (hidden / row_rms[:, None] * norm_gain).astype(jnp.bfloat16)
    logits = jnp.dot(
        lax.all_gather(normed, "tok", axis=0, tiled=True),
        unembed,
        preferred_element_type=jnp.float32,
    )
    softmax_top = lax.pmax(jnp.max(logits, axis=1), ("tok", "voc"))
    softmax_sum = lax.psum(jnp.sum(jnp.exp(logits - softmax_top[:, None]), axis=1), ("tok", "voc"))
    block_index = lax.axis_index("tok") * voc_count + lax.axis_index("voc")
    columns = block_index * voc_cols + jnp.arange(voc_cols, dtype=jnp.int32)
    onehot = (targets[:, None] == columns[None, :]).astype(jnp.float32)
    direction = (onehot - jnp.exp(logits - softmax_top[:, None]) / softmax_sum[:, None]).astype(
        jnp.bfloat16
    )
    grouped = direction.reshape(tok_count, tok_rows, voc_cols)
    weight_slabs = unembed.reshape(voc_count, slab_width, voc_cols)
    partial_term = jnp.einsum(
        "ikv,jdv->ijkd", grouped, weight_slabs, preferred_element_type=jnp.float32
    )
    partial_term = partial_term.reshape(tok_count * voc_count * tok_rows, slab_width)
    grad_normed = lax.psum_scatter(partial_term, ("tok", "voc"), scatter_dimension=0, tiled=True)
    offset = lax.axis_index("voc") * slab_width
    unit_part = lax.dynamic_slice_in_dim(hidden, offset, slab_width, 1) / row_rms[:, None]
    gain_part = lax.dynamic_slice_in_dim(norm_gain, offset, slab_width, 0)
    scaled = grad_normed * gain_part
    picked = decoder[:, feat_ids.reshape(-1)].astype(jnp.float32)
    inner_sum = lax.psum(jnp.sum(unit_part * scaled, axis=1), "voc")
    grad_resid = (scaled - unit_part * (inner_sum / model_width)[:, None]) / row_rms[:, None]
    projected = project_columns(picked, grad_resid, tok_rows, active)
    projected = lax.psum(projected, "voc")
    return projected * feat_acts


def solution(mesh):
    placed = (
        P("tok", None),
        P(),
        P(None, ("tok", "voc")),
        P(),
        P("tok", None),
        P("tok", None),
        P("voc", None),
    )
    return jax.shard_map(
        on_device, mesh=mesh, in_specs=placed, out_specs=P("tok", None), check_vma=False
    )
```

profile of v0, /device:TPU:32, one launch (start us, length us, event | category | flops | bytes accessed | tf_op | source)
XLA Modules:
  0.0 1611.4 jit_solution(8541509727573097663)
XLA Ops:
  6.5 0.0 all-gather.2.cloned.1.call-start
  6.5 1.1 multiply_reduce_fusion
  7.6 1.8 multiply_convert_fusion
  9.4 0.0 all-gather.2.cloned.1.call-update
  9.4 0.0 reduce-scatter.2.cloned.1.call-start
  9.5 0.0 copy-start.3
  9.5 42.0 %all-gather.2.cloned.1.call-done = bf16[512,3584]{1,0:T(8,128)(2,1)} async-done(((bf16[32,3584]{1,0:T(8,128)(2,1)}), bf16[512,3584]{1,0:T(8,128)(2,1)}) %all-gather.2.cloned.1.call-update) | async-done | bytes 3670032 | tf_op jit(solution)/shard_map/all_gather | solution.py:25
  51.5 6.8 fusion.2
  58.2 76.3 %pmax.7 = f32[512]{0:T(512)S(1)} all-reduce(f32[512]{0:T(512)S(1)} %get-tuple-element.5), channel_id=1, replica_groups=mesh['tok'=16,'voc'=16] {'tok','voc'}, use_global_device_ids=true, to_apply=%region_2.0 | all-reduce | flops 512 | bytes 4096 | tf_op jit(solution)/shard_map/pmax | solution.py:29
  134.6 0.4 fusion.1
  135.0 73.3 %psum.21 = f32[512]{0:T(512)S(1)} all-reduce(f32[512]{0:T(512)S(1)} %fusion.1), channel_id=1, replica_groups=mesh['tok'=16,'voc'=16] {'tok','voc'}, use_global_device_ids=true, to_apply=%region_4.0 | all-reduce | flops 512 | bytes 4096 | tf_op jit(solution)/shard_map/psum | solution.py:30
  208.3 0.0 copy-done.3
  208.3 0.5 subtract_convert_fusion
  208.8 8.3 fusion.3
  217.1 0.0 copy-start
  217.1 0.0 reduce-scatter.2.cloned.1.call-update
  217.2 0.9 copy-done
  218.1 0.8 dynamic_slice.6
  218.9 0.0 copy-start.2
  218.9 10.9 copy.8
  229.8 0.0 copy-done.2
  229.8 0.1 reshape.67
  229.9 0.0 copy-start.1
  229.9 11.1 gather_fusion
  241.0 1249.3 %reduce-scatter.2.cloned.1.call-done = f32[32,224]{1,0:T(8,128)} async-done(((f32[8192,224]{1,0:T(8,128)}), f32[32,224]{1,0:T(8,128)}) %reduce-scatter.2.cloned.1.call-update) | async-done | bytes 28688 | tf_op jit(solution)/shard_map/reduce_scatter | solution.py:43
  1490.3 0.9 multiply_reduce_fusion.1
  1491.2 43.3 %psum.22 = f32[32]{0:T(128)S(1)} all-reduce(f32[32]{0:T(128)S(1)} %multiply_reduce_fusion.1), channel_id=1, replica_groups=mesh['tok'=16,'voc'=16] {'voc'}, use_global_device_ids=true, to_apply=%region_7.0 | all-reduce | flops 32 | bytes 256 | tf_op jit(solution)/shard_map/psum | solution.py:49
  1534.5 0.8 divide_bitcast_fusion
  1535.4 0.4 fusion
  1535.7 0.1 reduce_sum.42
  1535.8 68.2 %psum.23 = f32[32,64]{1,0:T(8,128)S(1)} all-reduce(f32[32,64]{1,0:T(8,128)S(1)} %reduce_sum.42), channel_id=1, replica_groups=mesh['tok'=16,'voc'=16] {'voc'}, use_global_device_ids=true, to_apply=%region_9.0 | all-reduce | flops 2048 | bytes 16384 | tf_op jit(solution)/shard_map/psum | solution.py:52
  1604.0 0.0 copy-done.1
  1604.0 0.6 mul.61
  (6 shorter events, 0.1 us)
Async XLA Ops:
  6.5 45.0 %all-gather.2.cloned.1.call-start = ((), (), s32[]{:S(2)}) async-start(), calls=%async_computation.1 | async-start | bytes 3899392 | tf_op jit(solution)/shard_map/all_gather | solution.py:25
  9.4 1480.9 %reduce-scatter.2.cloned.1.call-start = ((), (), s32[]{:S(2)}) async-start(), calls=%async_computation.2 | async-start | bytes 8421376 | tf_op jit(solution)/shard_map/reduce_scatter | solution.py:43
  9.5 198.8 %copy-start.3 = (s32[512]{0:T(512)S(1)}, s32[512]{0:T(512)}, u32[]{:S(2)}) copy-start(s32[512]{0:T(512)} %param.10) | copy-start | bytes 6148
  217.1 0.9 copy-start
  218.9 10.9 copy-start.2
  229.9 1374.1 %copy-start.1 = (f32[32,64]{1,0:T(8,128)S(1)}, f32[32,64]{1,0:T(8,128)}, u32[]{:S(2)}) copy-start(f32[32,64]{1,0:T(8,128)} %param.12) | copy-start | bytes 24580
Sparse Core Ops, SparseCore 0:
  9.6 41.8 all-gather.1
  217.3 1272.9 reduce-scatter.1
where the time goes:
time: 1620 us; the launch traced here: 1610 us
  waiting for transfers between devices  1290 us (80%)
  blocking collectives  261 us (16%)
  local copies, waits for them, and re-layouts  23.8 us (1%)
    reduce_scatter x1, waiting for transfers between devices, on_device(): lax.psum_scatter(partial_term, ('tok', 'voc'), scatter_dimension=0, tiled...  1250 us
    pmax x1, blocking collectives, on_device(): softmax_top = lax.pmax(jnp.max(logits, axis=1), ('tok', 'voc'))  76.3 us
    psum x1, blocking collectives, on_device(): lax.psum(jnp.sum(jnp.exp(logits - softmax_top[:, None]), axis=1), ('tok',...  73.3 us
    psum x1, blocking collectives, on_device(): projected = lax.psum(projected, 'voc')  68.2 us
    psum x1, blocking collectives, on_device(): inner_sum = lax.psum(jnp.sum(unit_part * scaled, axis=1), 'voc')  43.3 us
    all_gather x1, waiting for transfers between devices, on_device(): lax.all_gather(normed, 'tok', axis=0, tiled=True)  42 us
  transfers between devices with their start and end apart: 2, of which 2 were waited for; matrix products, arithmetic and copies ran while one was open for 1% of the time, Pallas kernels for 0%

commit v1 on v0

v1 whole, which is shorter than its diff:
```python
import functools

import jax
import jax.numpy as jnp
from jax import lax
from jax.experimental import pallas as pl
from jax.experimental.pallas import tpu as pltpu
from jax.sharding import PartitionSpec as P

EPSILON = 1e-06
MESH = pl.DeviceIdType.MESH
F32 = jnp.float32
BF16 = jnp.bfloat16


def body(
    resid_ref, gain_ref, unembed_hbm, rel_ref, ids_ref, acts_ref, decoder_hbm,
    out_ref,
    w_ref, dec_ref, nall, ebuf, dirbuf, rms_ref, uslab, gslab, idbuf,
    st_own, st_in, acc, crecv, sx, sy, rx, ry, s2x, s2y, r2x, r2y, zs, zr,
    bz, az, fx_own, fx_in,
    load_sem, gy_s, gy_r, gx_s, gx_r, gc_s, gc_r, gd_s, gd_r, st_s, st_r,
    c_s, c_r, x1_s, x1_r, y1_s, y1_r, x2_s, x2_r, y2_s, y2_r, z_s, z_r,
    bz_s, bz_r, az_s, az_r, fx_s, fx_r,
):
    tok = lax.axis_index("tok")
    voc = lax.axis_index("voc")
    x_lo = tok // 8
    y = (tok // 2) % 4
    core = tok % 2
    x_hi = voc // 8
    z = voc % 8
    x = x_hi * 2 + x_lo

    def device(xx, yy, zz, cc):
        return ((xx % 2) * 8 + yy * 2 + cc, (xx // 2) * 8 + zz)

    def x_peer(k):
        return device((x + k) % 4, y, z, core)

    def y_peer(k):
        return device(x, (y + k) % 4, z, core)

    def z_peer(k):
        return device(x, y, (z + k) % 8, core)

    sibling = device(x, y, z, 1 - core)

    def send(src, dst, s, r, peer):
        return pltpu.make_async_remote_copy(
            src_ref=src, dst_ref=dst, send_sem=s, recv_sem=r, device_id=peer, device_id_type=MESH
        )

    load_w = pltpu.make_async_copy(unembed_hbm, w_ref, load_sem.at[0])
    load_d = pltpu.make_async_copy(decoder_hbm, dec_ref, load_sem.at[1])
    load_w.start()
    load_d.start()
    barrier = pltpu.get_barrier_semaphore()
    peers = [sibling]
    peers += [x_peer(k) for k in (1, 2, 3)]
    peers += [y_peer(k) for k in (1, 2, 3)]
    peers += [z_peer(k) for k in range(1, 8)]
    for peer in peers:
        pl.semaphore_signal(barrier, inc=1, device_id=peer, device_id_type=MESH)

    hidden = resid_ref[...].astype(F32)
    width = hidden.shape[1]
    rms = jnp.sqrt(jnp.mean(hidden * hidden, axis=1, keepdims=True) + EPSILON)
    rms_ref[...] = jnp.broadcast_to(rms, rms_ref.shape)
    nall[x_lo, core, y] = (hidden / rms * gain_ref[...]).astype(BF16)

    half = width // 2
    slab = half // 8
    start = pl.multiple_of(x_hi * half, half)
    unit_half = resid_ref[:, pl.ds(start, half)].astype(F32) / rms
    gain_half = gain_ref[:, pl.ds(start, half)]
    for zz in range(8):
        @pl.when(z == zz)
        def _():
            uslab[...] = unit_half[:, zz * slab:(zz + 1) * slab]
            gslab[...] = gain_half[:, zz * slab:(zz + 1) * slab]
    idbuf[...] = jnp.zeros_like(idbuf)
    idbuf[:, 0:64] = ids_ref[...]

    pl.semaphore_wait(barrier, len(peers))

    def gy(k):
        part = nall.at[x_lo, core, y]
        return send(part, part, gy_s.at[k - 1], gy_r.at[k - 1], y_peer(k))

    def gx(kb, d):
        part = nall.at[x_lo, core, (y - kb + 4) % 4, pl.ds(16 * d, 16)]
        return send(part, part, gx_s.at[kb, d], gx_r.at[kb, d], x_peer(1 if d == 0 else 3))

    def gc(kb):
        part = nall.at[x_lo, core, (y - kb + 4) % 4]
        return send(part, part, gc_s.at[kb], gc_r.at[kb], sibling)

    def gd(kb):
        part = nall.at[1 - x_lo, core, (y - kb + 4) % 4]
        return send(part, part, gd_s.at[kb], gd_r.at[kb], sibling)

    for k in (1, 3, 2):
        gy(k).start()
    gx(0, 0).start()
    gx(0, 1).start()
    gc(0).start()

    def attribute(values):
        high = values.astype(BF16)
        low = (values - high.astype(F32)).astype(BF16)
        stacked = jnp.concatenate([high, low], axis=0)
        lanes = jnp.bitwise_and(idbuf[...], 127)
        tiles = jnp.right_shift(idbuf[...], 7)

        def step(n, picked):
            cols = pl.ds(pl.multiple_of(n * 1024, 1024), 1024)
            both = jnp.dot(stacked, dec_ref[:, cols], preferred_element_type=F32)
            dots = both[0:32] + both[32:64]
            for q in range(8):
                got = jnp.take_along_axis(
                    dots[:, q * 128:(q + 1) * 128], lanes, axis=1, mode="promise_in_bounds"
                )
                picked = jnp.where(tiles == n * 8 + q, got, picked)
            return picked

        return lax.fori_loop(0, dec_ref.shape[1] // 1024, step, jnp.zeros((32, 128), F32))

    def to_voc(buf, s, r):
        return [send(buf.at[z], buf.at[z], s.at[k - 1], r.at[k - 1], z_peer(k)) for k in range(1, 8)]

    load_d.wait()
    bz[z] = attribute(uslab[...])
    for copy in to_voc(bz, bz_s, bz_r):
        copy.start()

    for k in (1, 3, 2):
        gy(k).wait_recv()
        gx(k, 0).start()
        gx(k, 1).start()
        gc(k).start()

    load_w.wait()

    eye = lax.broadcasted_iota(jnp.int32, (128, 128), 0) == lax.broadcasted_iota(jnp.int32, (128, 128), 1)

    def to_row(col):
        return jnp.sum(jnp.where(eye, col, 0.0), axis=0, keepdims=True)

    def to_col(row):
        return jnp.sum(jnp.where(eye, row, 0.0), axis=1, keepdims=True)

    def logits_of(xl):
        def step(n, carry):
            cols = pl.ds(pl.multiple_of(n * 256, 256), 256)
            left = nall[xl].reshape(256, width)
            ebuf[xl, :, cols] = jnp.dot(left, w_ref[:, cols], preferred_element_type=F32)
            return carry

        lax.fori_loop(0, ebuf.shape[2] // 256, step, 0)
        for q in range(2):
            rows = pl.ds(q * 128, 128)
            part = ebuf[xl, rows]
            top = jnp.max(part, axis=1, keepdims=True)
            part = jnp.exp(part - top)
            ebuf[xl, rows] = part
            st_own[0, pl.ds(xl * 2 + q, 1)] = to_row(top)
            st_own[0, pl.ds(4 + xl * 2 + q, 1)] = to_row(jnp.sum(part, axis=1, keepdims=True))

    for k in (0, 1, 3, 2):
        gc(k).wait_recv()
    logits_of(x_lo)
    for k in (0, 1, 3, 2):
        gx(k, 0).wait_recv()
        gx(k, 1).wait_recv()
        gd(k).start()
    for k in (0, 1, 3, 2):
        gd(k).wait_recv()
    logits_of(1 - x_lo)

    own = st_own[0]
    top, total = own[0:4], own[4:8]
    first_top = top
    groups = [peers[0:1], peers[1:4], peers[4:7], peers[7:14]]
    index = 0
    for stage, group in enumerate(groups):
        if stage > 0:
            st_own[stage, 0:4] = top
            st_own[stage, 4:8] = total
        copies = []
        for peer in group:
            copies.append(send(st_own.at[stage], st_in.at[index], st_s.at[index], st_r.at[index], peer))
            copies[-1].start()
            index += 1
        tiles = [(top, total)]
        for n, copy in enumerate(copies):
            copy.wait_recv()
            got = st_in[index - len(copies) + n]
            tiles.append((got[0:4], got[4:8]))
        merged = functools.reduce(jnp.maximum, [t for t, _ in tiles])
        total = sum(s * jnp.exp(t - merged) for t, s in tiles)
        top = merged
    scale = jnp.exp(first_top - top) / total
    voc_cols = w_ref.shape[1]
    lane = lax.broadcasted_iota(jnp.int32, (128, voc_cols), 1).astype(F32)
    for q in range(4):
        prob = ebuf[q // 2, pl.ds((q % 2) * 128, 128)] * to_col(scale[q:q + 1])
        hot = jnp.where(lane == to_col(rel_ref[q:q + 1, :]), 1.0, 0.0)
        dirbuf[pl.ds(q * 128, 128)] = (hot - prob).astype(BF16)

    def c_copy(j):
        return send(acc.at[1 - core, j], crecv.at[j], c_s.at[j], c_r.at[j], sibling)

    def x1(j, k):
        to = (x + k) % 4
        return send(sx.at[j, to // 2, to % 2], rx.at[j, k - 1], x1_s.at[j, k - 1], x1_r.at[j, k - 1], x_peer(k))

    def y1(j, k):
        return send(sy.at[j, (y + k) % 4], ry.at[j, k - 1], y1_s.at[j, k - 1], y1_r.at[j, k - 1], y_peer(k))

    def x2(j, k):
        to = (x + k) % 4
        return send(s2x.at[j, to // 2, to % 2], r2x.at[j, k - 1], x2_s.at[j, k - 1], x2_r.at[j, k - 1], x_peer(k))

    def y2(j, k):
        return send(s2y.at[j, (y + k) % 4], r2y.at[j, k - 1], y2_s.at[j, k - 1], y2_r.at[j, k - 1], y_peer(k))

    def z3(j):
        return send(zs.at[j], zr.at[j], z_s.at[j], z_r.at[j], z_peer(j + 1))

    def pipeline(i, carry):
        @pl.when(i < 8)
        def _():
            group = (z + 1 + i) % 8
            for hx in range(2):
                rows = pl.ds(pl.multiple_of(hx * half + group * slab, 32), slab)
                part = lax.dot_general(
                    dirbuf[...], w_ref[rows, :], (((1,), (1,)), ((), ())), preferred_element_type=F32
                )
                for q in range(4):
                    acc[q % 2, i, hx, q // 2] = part[q * 128:(q + 1) * 128].reshape(4, 32, slab)
            c_copy(i).start()

        @pl.when((i >= 1) & (i < 9))
        def _():
            j = i - 1
            c_copy(j).wait_recv()
            for hx in range(2):
                for xl in range(2):
                    both = acc[core, j, hx, xl] + crecv[j, hx, xl]
                    acc[core, j, hx, xl] = both
                    sx[j, hx, xl] = both[:, 0:16].astype(BF16)
                    for yy in range(4):
                        sy[j, yy, hx, xl] = both[yy, 16:32].astype(BF16)
            for k in (2, 1, 3):
                x1(j, k).start()
                y1(j, k).start()

        @pl.when((i >= 3) & (i < 11))
        def _():
            j = i - 3
            for k in (1, 2, 3):
                x1(j, k).wait_recv()
            mine = acc[core, j, x_hi, x_lo, :, 0:16]
            for k in range(3):
                mine = mine + rx[j, k].astype(F32)
            s2y[j] = mine
            for k in (2, 1, 3):
                y2(j, k).start()
            for k in (1, 2, 3):
                y1(j, k).wait_recv()
            other = acc[core, j, :, :, y, 16:32]
            for k in range(3):
                other = other + ry[j, k].astype(F32)
            s2x[j] = other
            for k in (2, 1, 3):
                x2(j, k).start()

        @pl.when(i >= 5)
        def _():
            j = i - 5
            for k in (1, 2, 3):
                y2(j, k).wait_recv()
            upper = s2y[j, y]
            for k in range(3):
                upper = upper + r2y[j, k]
            zs[j, 0:16] = upper
            for k in (1, 2, 3):
                x2(j, k).wait_recv()
            lower = s2x[j, x_hi, x_lo]
            for k in range(3):
                lower = lower + r2x[j, k]
            zs[j, 16:32] = lower

            @pl.when(j < 7)
            def _():
                z3(j).start()

        return carry

    lax.fori_loop(0, 13, pipeline, 0)
    grad = zs[7]
    for j in range(7):
        z3(j).wait_recv()
        grad = grad + zr[j]

    scaled = grad * gslab[...]
    inner = jnp.sum(uslab[...] * scaled, axis=1, keepdims=True)
    picked = attribute(scaled)
    lane = lax.broadcasted_iota(jnp.int32, (32, 128), 1)
    az[z] = jnp.where(lane < 64, picked, inner)
    for copy in to_voc(az, az_s, az_r):
        copy.start()
    for copy in to_voc(bz, bz_s, bz_r):
        copy.wait_recv()
    for copy in to_voc(az, az_s, az_r):
        copy.wait_recv()
    fx_own[0] = sum(az[n] for n in range(8))
    fx_own[1] = sum(bz[n] for n in range(8))
    last = send(fx_own, fx_in, fx_s.at[0], fx_r.at[0], x_peer(2))
    last.start()
    last.wait_recv()
    both = fx_own[0] + fx_in[0]
    unit_dot = fx_own[1] + fx_in[1]
    mean = both[:, 64:65] * (1.0 / width)
    out_ref[...] = ((both - unit_dot * mean) / rms_ref[...])[:, 0:64] * acts_ref[...]

    for k in (1, 2, 3):
        gy(k).wait_send()
    for k in range(4):
        gx(k, 0).wait_send()
        gx(k, 1).wait_send()
        gc(k).wait_send()
        gd(k).wait_send()
    index = 0
    for stage, group in enumerate(groups):
        for peer in group:
            send(st_own.at[stage], st_in.at[index], st_s.at[index], st_r.at[index], peer).wait_send()
            index += 1

    def drain(j, carry):
        c_copy(j).wait_send()
        for k in (1, 2, 3):
            x1(j, k).wait_send()
            y1(j, k).wait_send()
            x2(j, k).wait_send()
            y2(j, k).wait_send()

        @pl.when(j < 7)
        def _():
            z3(j).wait_send()

        return carry

    lax.fori_loop(0, 8, drain, 0)
    for copy in to_voc(bz, bz_s, bz_r) + to_voc(az, az_s, az_r):
        copy.wait_send()
    last.wait_send()


def on_device(resid, norm_gain, unembed, targets, feat_ids, feat_acts, decoder):
    width = resid.shape[1]
    voc_cols = unembed.shape[1]
    slab, features = decoder.shape
    block_index = lax.axis_index("tok") * 16 + lax.axis_index("voc")
    rel = (targets - block_index * voc_cols).astype(F32)
    rel = rel.reshape(2, 4, 2, 32).transpose(0, 2, 1, 3).reshape(4, 128)
    vm = pl.BlockSpec(memory_space=pltpu.VMEM)
    hbm = pl.BlockSpec(memory_space=pl.ANY)
    dma = pltpu.SemaphoreType.DMA
    return pl.pallas_call(
        body,
        out_shape=jax.ShapeDtypeStruct(feat_acts.shape, F32),
        in_specs=[vm, vm, hbm, vm, vm, vm, hbm],
        out_specs=vm,
        scratch_shapes=[
            pltpu.VMEM(unembed.shape, BF16),
            pltpu.VMEM(decoder.shape, BF16),
            pltpu.VMEM((2, 2, 4, 32, width), BF16),
            pltpu.VMEM((2, 256, voc_cols), F32),
            pltpu.VMEM((512, voc_cols), BF16),
            pltpu.VMEM((32, 128), F32),
            pltpu.VMEM((32, slab), F32),
            pltpu.VMEM((1, slab), F32),
            pltpu.VMEM((32, 128), jnp.int32),
            pltpu.VMEM((4, 8, 128), F32),
            pltpu.VMEM((14, 8, 128), F32),
            pltpu.VMEM((2, 8, 2, 2, 4, 32, slab), F32),
            pltpu.VMEM((8, 2, 2, 4, 32, slab), F32),
            pltpu.VMEM((8, 2, 2, 4, 16, slab), BF16),
            pltpu.VMEM((8, 4, 2, 2, 16, slab), BF16),
            pltpu.VMEM((8, 3, 4, 16, slab), BF16),
            pltpu.VMEM((8, 3, 2, 2, 16, slab), BF16),
            pltpu.VMEM((8, 2, 2, 16, slab), F32),
            pltpu.VMEM((8, 4, 16, slab), F32),
            pltpu.VMEM((8, 3, 16, slab), F32),
            pltpu.VMEM((8, 3, 16, slab), F32),
            pltpu.VMEM((8, 32, slab), F32),
            pltpu.VMEM((7, 32, slab), F32),
            pltpu.VMEM((8, 32, 128), F32),
            pltpu.VMEM((8, 32, 128), F32),
            pltpu.VMEM((2, 32, 128), F32),
            pltpu.VMEM((2, 32, 128), F32),
            dma((2,)),
            dma((3,)), dma((3,)),
            dma((4, 2)), dma((4, 2)),
            dma((4,)), dma((4,)),
            dma((4,)), dma((4,)),
            dma((14,)), dma((14,)),
            dma((8,)), dma((8,)),
            dma((8, 3)), dma((8, 3)),
            dma((8, 3)), dma((8, 3)),
            dma((8, 3)), dma((8, 3)),
            dma((8, 3)), dma((8, 3)),
            dma((7,)), dma((7,)),
            dma((7,)), dma((7,)),
            dma((7,)), dma((7,)),
            dma((1,)), dma((1,)),
        ],
        compiler_params=pltpu.CompilerParams(
            collective_id=0, has_side_effects=True, vmem_limit_bytes=60 * 1024 * 1024
        ),
    )(resid, norm_gain.reshape(1, width), unembed, rel, feat_ids, feat_acts, decoder)


def solution(mesh):
    placed = (
        P("tok", None),
        P(),
        P(None, ("tok", "voc")),
        P(),
        P("tok", None),
        P("tok", None),
        P("voc", None),
    )
    return jax.shard_map(
        on_device, mesh=mesh, in_specs=placed, out_specs=P("tok", None), check_vma=False
    )
```

time: 1620 us -> 90.7 us (0.06)
  waiting for transfers between devices: 1290 us -> 0 us
  blocking collectives: 261 us -> 0 us
  Pallas kernels: 0 us -> 85.5 us
  local copies, waits for them, and re-layouts: 23.8 us -> 3.42 us
    reduce_scatter x1 -> x0, waiting for transfers between devices: 1250 us -> none  [on_device(): lax.psum_scatter(partial_term, ('tok', 'voc'), scatter_dimension=0, tiled...]
    psum x3 -> x0, blocking collectives: 185 us -> none  [the longest x1 73.3 us: on_device(): lax.psum(jnp.sum(jnp.exp(logits - softmax_top[:, None]), axis=1), ('tok',...]
    pallas_call x0 -> x1, Pallas kernels: none -> 85.5 us  [on_device(): pl.pallas_call(body, out_shape=jax.ShapeDtypeStruct(feat_acts.shape, F32)...]
    pmax x1 -> x0, blocking collectives: 76.3 us -> none  [on_device(): softmax_top = lax.pmax(jnp.max(logits, axis=1), ('tok', 'voc'))]
    all_gather x1 -> x0, waiting for transfers between devices: 42 us -> none  [on_device(): lax.all_gather(normed, 'tok', axis=0, tiled=True)]
  transfers between devices with their start and end apart: 2 -> 0, of which waited for: 2 -> 0; matrix products, arithmetic and copies ran while one was open for 1% -> 0% of each run, Pallas kernels for 0% -> 0%
where the time goes in v1:
time: 90.7 us; the launch traced here: 89.6 us
  Pallas kernels  85.5 us (94%)
  local copies, waits for them, and re-layouts  3.42 us (4%)
    pallas_call x1, Pallas kernels, on_device(): pl.pallas_call(body, out_shape=jax.ShapeDtypeStruct(feat_acts.shape, F32)...  85.5 us

profile of v1, /device:TPU:32, one launch (start us, length us, event | category | flops | bytes accessed | tf_op | source)
XLA Modules:
  0.0 89.6 jit_solution(451594581684269300)
XLA Ops:
  0.0 0.7 subtract_convert_fusion
  0.7 0.1 reshape.10
  0.8 0.7 reshape.11.rel_ref
  1.5 1.3 %reshape.9.gain_ref = f32[1,3584]{1,0:T(1,128)} reshape(f32[3584]{0:T(1024)} %param.8) | data formatting | bytes 28672 | tf_op jit(solution)/shard_map/reshape | solution.py:423
  2.8 85.5 %shard_map.73 = f32[32,64]{1,0:T(8,128)} custom-call(bf16[32,3584]{1,0:T(8,128)(2,1)} %resid_ref.1, f32[1,3584]{1,0:T(1,128)} %reshape.9.gain_ref, bf16[3584,768]{1,0:T(8,128)(2,1)} %unembed_hbm.1, f32[4,128]{1,0:T(4,128)} %reshape.11.rel_ref, s32[32,64]{1,0:T(8,128)} %ids_ref.1, f32[32,64]{1,0:T(8,128)} %acts_ref.1, bf16[224,16384]{1,0:T(8,128)(2,1)} %decoder_hbm.1), custom_call_target="tpu_custom_call" | custom-call | tf_op jit(solution)/shard_map/pallas_call | solution.py:371
  88.3 1.3 %copy.10 = f32[32,64]{1,0:T(8,128)} copy(f32[32,64]{1,0:T(8,128)} %shard_map.73) | data formatting | bytes 16384
  (1 shorter events, 0.0 us)

commit v2 on v1

--- a/solution.py
+++ b/solution.py
@@ -14,14 +14,14 @@
 
 
 def body(
-    resid_ref, gain_ref, unembed_hbm, rel_ref, ids_ref, acts_ref, decoder_hbm,
+    resid_ref, gain_ref, unembed_hbm, targets_ref, ids_ref, decoder_hbm,
     out_ref,
-    w_ref, dec_ref, nall, ebuf, dirbuf, rms_ref, uslab, gslab, idbuf,
+    w_ref, dec_ref, nall, ebuf, dirbuf, rms_ref, gain_buf, uslab, gslab, idbuf,
     st_own, st_in, acc, crecv, sx, sy, rx, ry, s2x, s2y, r2x, r2y, zs, zr,
-    bz, az, fx_own, fx_in,
+    bz, az, iz, bx, ax, ix,
     load_sem, gy_s, gy_r, gx_s, gx_r, gc_s, gc_r, gd_s, gd_r, st_s, st_r,
     c_s, c_r, x1_s, x1_r, y1_s, y1_r, x2_s, x2_r, y2_s, y2_r, z_s, z_r,
-    bz_s, bz_r, az_s, az_r, fx_s, fx_r,
+    bz_s, bz_r, az_s, az_r, iz_s, iz_r, fx_s, fx_r,
 ):
     tok = lax.axis_index("tok")
     voc = lax.axis_index("voc")
@@ -67,13 +67,15 @@
     width = hidden.shape[1]
     rms = jnp.sqrt(jnp.mean(hidden * hidden, axis=1, keepdims=True) + EPSILON)
     rms_ref[...] = jnp.broadcast_to(rms, rms_ref.shape)
-    nall[x_lo, core, y] = (hidden / rms * gain_ref[...]).astype(BF16)
+    gain = gain_ref[...].reshape(1, width)
+    gain_buf[...] = gain
+    nall[x_lo, core, y] = (hidden / rms * gain).astype(BF16)
 
     half = width // 2
     slab = half // 8
     start = pl.multiple_of(x_hi * half, half)
     unit_half = resid_ref[:, pl.ds(start, half)].astype(F32) / rms
-    gain_half = gain_ref[:, pl.ds(start, half)]
+    gain_half = gain_buf[:, pl.ds(start, half)]
     for zz in range(8):
         @pl.when(z == zz)
         def _():
@@ -105,6 +107,8 @@
     gx(0, 0).start()
     gx(0, 1).start()
     gc(0).start()
+
+    low_half = lax.broadcasted_iota(jnp.int32, (16, 128), 1) < 64
 
     def attribute(values):
         high = values.astype(BF16)
@@ -124,7 +128,8 @@
                 picked = jnp.where(tiles == n * 8 + q, got, picked)
             return picked
 
-        return lax.fori_loop(0, dec_ref.shape[1] // 1024, step, jnp.zeros((32, 128), F32))
+        picked = lax.fori_loop(0, dec_ref.shape[1] // 1024, step, jnp.zeros((32, 128), F32))
+        return jnp.where(low_half, picked[0:16], pltpu.roll(picked[16:32], 64, 1))
 
     def to_voc(buf, s, r):
         return [send(buf.at[z], buf.at[z], s.at[k - 1], r.at[k - 1], z_peer(k)) for k in range(1, 8)]
@@ -203,10 +208,27 @@
     scale = jnp.exp(first_top - top) / total
     voc_cols = w_ref.shape[1]
     lane = lax.broadcasted_iota(jnp.int32, (128, voc_cols), 1).astype(F32)
+    rel = (targets_ref[...] - (tok * 16 + voc) * voc_cols).astype(F32)
+    cols = [to_col(rel[n:n + 1]) for n in range(4)]
     for q in range(4):
         prob = ebuf[q // 2, pl.ds((q % 2) * 128, 128)] * to_col(scale[q:q + 1])
-        hot = jnp.where(lane == to_col(rel_ref[q:q + 1, :]), 1.0, 0.0)
+        parts = []
+        for yy in range(4):
+            first = (yy % 2) * 64 + (q % 2) * 32
+            parts.append(cols[(q // 2) * 2 + yy // 2][first:first + 32])
+        hot = jnp.where(lane == jnp.concatenate(parts, axis=0), 1.0, 0.0)
         dirbuf[pl.ds(q * 128, 128)] = (hot - prob).astype(BF16)
+
+    def cross(buf, n):
+        return send(buf.at[0], buf.at[1], fx_s.at[n], fx_r.at[n], x_peer(2))
+
+    def add_voc(buf, s, r, over, n):
+        for copy in to_voc(buf, s, r):
+            copy.wait_recv()
+        over[0] = sum(buf[m] for m in range(8))
+        cross(over, n).start()
+
+    add_voc(bz, bz_s, bz_r, bx, 0)
 
     def c_copy(j):
         return send(acc.at[1 - core, j], crecv.at[j], c_s.at[j], c_r.at[j], sibling)
@@ -264,7 +286,8 @@
             mine = acc[core, j, x_hi, x_lo, :, 0:16]
             for k in range(3):
                 mine = mine + rx[j, k].astype(F32)
-            s2y[j] = mine
+            acc[core, j, x_hi, x_lo, :, 0:16] = mine
+            s2y[j] = mine.astype(BF16)
             for k in (2, 1, 3):
                 y2(j, k).start()
             for k in (1, 2, 3):
@@ -272,7 +295,8 @@
             other = acc[core, j, :, :, y, 16:32]
             for k in range(3):
                 other = other + ry[j, k].astype(F32)
-            s2x[j] = other
+            acc[core, j, :, :, y, 16:32] = other
+            s2x[j] = other.astype(BF16)
             for k in (2, 1, 3):
                 x2(j, k).start()
 
@@ -281,15 +305,15 @@
             j = i - 5
             for k in (1, 2, 3):
                 y2(j, k).wait_recv()
-            upper = s2y[j, y]
+            upper = acc[core, j, x_hi, x_lo, y, 0:16]
             for k in range(3):
-                upper = upper + r2y[j, k]
+                upper = upper + r2y[j, k].astype(F32)
             zs[j, 0:16] = upper
             for k in (1, 2, 3):
                 x2(j, k).wait_recv()
-            lower = s2x[j, x_hi, x_lo]
+            lower = acc[core, j, x_hi, x_lo, y, 16:32]
             for k in range(3):
-                lower = lower + r2x[j, k]
+                lower = lower + r2x[j, k].astype(F32)
             zs[j, 16:32] = lower
 
             @pl.when(j < 7)
@@ -306,24 +330,27 @@
 
     scaled = grad * gslab[...]
     inner = jnp.sum(uslab[...] * scaled, axis=1, keepdims=True)
-    picked = attribute(scaled)
-    lane = lax.broadcasted_iota(jnp.int32, (32, 128), 1)
-    az[z] = jnp.where(lane < 64, picked, inner)
+    iz[z] = jnp.broadcast_to(inner, (32, 128))
+    for copy in to_voc(iz, iz_s, iz_r):
+        copy.start()
+    az[z] = attribute(scaled)
     for copy in to_voc(az, az_s, az_r):
         copy.start()
-    for copy in to_voc(bz, bz_s, bz_r):
-        copy.wait_recv()
-    for copy in to_voc(az, az_s, az_r):
-        copy.wait_recv()
-    fx_own[0] = sum(az[n] for n in range(8))
-    fx_own[1] = sum(bz[n] for n in range(8))
-    last = send(fx_own, fx_in, fx_s.at[0], fx_r.at[0], x_peer(2))
-    last.start()
-    last.wait_recv()
-    both = fx_own[0] + fx_in[0]
-    unit_dot = fx_own[1] + fx_in[1]
-    mean = both[:, 64:65] * (1.0 / width)
-    out_ref[...] = ((both - unit_dot * mean) / rms_ref[...])[:, 0:64] * acts_ref[...]
+    add_voc(iz, iz_s, iz_r, ix, 1)
+    add_voc(az, az_s, az_r, ax, 2)
+    cross(bx, 0).wait_recv()
+    cross(ix, 1).wait_recv()
+    unit_dot = bx[0] + bx[1]
+    mean = (ix[0] + ix[1]) * (1.0 / width)
+    scale = 1.0 / rms_ref[...]
+    cross(ax, 2).wait_recv()
+    both = ax[0] + ax[1]
+    for n in range(2):
+        rows = slice(n * 16, n * 16 + 16)
+        if n == 1:
+            both = pltpu.roll(both, 64, 1)
+            unit_dot = pltpu.roll(unit_dot, 64, 1)
+        out_ref[rows] = ((both - unit_dot * mean[rows]) * scale[rows])[:, 0:64]
 
     for k in (1, 2, 3):
         gy(k).wait_send()
@@ -353,25 +380,23 @@
         return carry
 
     lax.fori_loop(0, 8, drain, 0)
-    for copy in to_voc(bz, bz_s, bz_r) + to_voc(az, az_s, az_r):
+    for copy in to_voc(bz, bz_s, bz_r) + to_voc(az, az_s, az_r) + to_voc(iz, iz_s, iz_r):
         copy.wait_send()
-    last.wait_send()
+    for n, over in enumerate((bx, ix, ax)):
+        cross(over, n).wait_send()
 
 
 def on_device(resid, norm_gain, unembed, targets, feat_ids, feat_acts, decoder):
     width = resid.shape[1]
     voc_cols = unembed.shape[1]
     slab, features = decoder.shape
-    block_index = lax.axis_index("tok") * 16 + lax.axis_index("voc")
-    rel = (targets - block_index * voc_cols).astype(F32)
-    rel = rel.reshape(2, 4, 2, 32).transpose(0, 2, 1, 3).reshape(4, 128)
     vm = pl.BlockSpec(memory_space=pltpu.VMEM)
     hbm = pl.BlockSpec(memory_space=pl.ANY)
     dma = pltpu.SemaphoreType.DMA
-    return pl.pallas_call(
+    projected = pl.pallas_call(
         body,
         out_shape=jax.ShapeDtypeStruct(feat_acts.shape, F32),
-        in_specs=[vm, vm, hbm, vm, vm, vm, hbm],
+        in_specs=[vm, vm, hbm, vm, vm, hbm],
         out_specs=vm,
         scratch_shapes=[
             pltpu.VMEM(unembed.shape, BF16),
@@ -380,6 +405,7 @@
             pltpu.VMEM((2, 256, voc_cols), F32),
             pltpu.VMEM((512, voc_cols), BF16),
             pltpu.VMEM((32, 128), F32),
+            pltpu.VMEM((1, width), F32),
             pltpu.VMEM((32, slab), F32),
             pltpu.VMEM((1, slab), F32),
             pltpu.VMEM((32, 128), jnp.int32),
@@ -391,15 +417,17 @@
             pltpu.VMEM((8, 4, 2, 2, 16, slab), BF16),
             pltpu.VMEM((8, 3, 4, 16, slab), BF16),
             pltpu.VMEM((8, 3, 2, 2, 16, slab), BF16),
-            pltpu.VMEM((8, 2, 2, 16, slab), F32),
-            pltpu.VMEM((8, 4, 16, slab), F32),
-            pltpu.VMEM((8, 3, 16, slab), F32),
-            pltpu.VMEM((8, 3, 16, slab), F32),
+            pltpu.VMEM((8, 2, 2, 16, slab), BF16),
+            pltpu.VMEM((8, 4, 16, slab), BF16),
+            pltpu.VMEM((8, 3, 16, slab), BF16),
+            pltpu.VMEM((8, 3, 16, slab), BF16),
             pltpu.VMEM((8, 32, slab), F32),
             pltpu.VMEM((7, 32, slab), F32),
+            pltpu.VMEM((8, 16, 128), F32),
+            pltpu.VMEM((8, 16, 128), F32),
             pltpu.VMEM((8, 32, 128), F32),
-            pltpu.VMEM((8, 32, 128), F32),
-            pltpu.VMEM((2, 32, 128), F32),
+            pltpu.VMEM((2, 16, 128), F32),
+            pltpu.VMEM((2, 16, 128), F32),
             pltpu.VMEM((2, 32, 128), F32),
             dma((2,)),
             dma((3,)), dma((3,)),
@@ -415,12 +443,14 @@
             dma((7,)), dma((7,)),
             dma((7,)), dma((7,)),
             dma((7,)), dma((7,)),
-            dma((1,)), dma((1,)),
+            dma((7,)), dma((7,)),
+            dma((3,)), dma((3,)),
         ],
         compiler_params=pltpu.CompilerParams(
             collective_id=0, has_side_effects=True, vmem_limit_bytes=60 * 1024 * 1024
         ),
-    )(resid, norm_gain.reshape(1, width), unembed, rel, feat_ids, feat_acts, decoder)
+    )(resid, norm_gain, unembed, targets.reshape(4, 128), feat_ids, decoder)
+    return projected * feat_acts
 
 
 def solution(mesh):

time: 90.7 us -> 85.6 us (0.944)
  local copies, waits for them, and re-layouts: 3.42 us -> 0.01 us
  Pallas kernels: 85.5 us -> 83.3 us
    pallas_call x1, Pallas kernels: 85.5 us -> 83.3 us  [on_device(): pl.pallas_call(body, out_shape=jax.ShapeDtypeStruct(feat_acts.shape, F32)...]
    reshape x3 -> x0, local copies, waits for them, and re-layouts: 2.09 us -> none  [the longest x1 1.33 us: on_device(): norm_gain.reshape(1, width)]
    mul x0 -> x1, other arithmetic: none -> 1.33 us  [on_device(): return projected * feat_acts]
    unnamed x1 -> x2, local copies, waits for them, and re-layouts: 1.32 us -> 0.01 us
where the time goes in v2:
time: 85.6 us; the launch traced here: 84.7 us
  Pallas kernels  83.3 us (97%)
  other arithmetic  1.33 us (2%)
    pallas_call x1, Pallas kernels, on_device(): pl.pallas_call(body, out_shape=jax.ShapeDtypeStruct(feat_acts.shape, F32)...  83.3 us

profile of v2, /device:TPU:32, one launch (start us, length us, event | category | flops | bytes accessed | tf_op | source)
XLA Modules:
  0.0 84.7 jit_solution(14998179082864323903)
XLA Ops:
  0.0 0.0 copy-start
  0.0 83.3 %shard_map.73 = f32[32,64]{1,0:T(8,128)} custom-call(bf16[32,3584]{1,0:T(8,128)(2,1)} %resid_ref.1, f32[3584]{0:T(1024)} %gain_ref.1, bf16[3584,768]{1,0:T(8,128)(2,1)} %unembed_hbm.1, s32[4,128]{1,0:T(4,128)} %bitcast.1, s32[32,64]{1,0:T(8,128)} %ids_ref.1, bf16[224,16384]{1,0:T(8,128)(2,1)} %decoder_hbm.1), custom_call_target="tpu_custom_call" | custom-call | tf_op jit(solution)/shard_map/pallas_call | solution.py:396
  83.3 0.0 copy-done
  83.3 1.3 %mul.3 = f32[32,64]{1,0:T(8,128)} multiply(f32[32,64]{1,0:T(8,128)} %shard_map.73, f32[32,64]{1,0:T(8,128)S(1)} %copy-done) | non-fusion elementwise | flops 2048 | bytes 24576 | tf_op jit(solution)/shard_map/mul | solution.py:453
Async XLA Ops:
  0.0 83.3 %copy-start = (f32[32,64]{1,0:T(8,128)S(1)}, f32[32,64]{1,0:T(8,128)}, u32[]{:S(2)}) copy-start(f32[32,64]{1,0:T(8,128)} %param.12) | copy-start | bytes 24580

commit v3 on v2

v3 whole, which is shorter than its diff:
```python
import functools

import jax
import jax.numpy as jnp
from jax import lax
from jax.experimental import pallas as pl
from jax.experimental.pallas import tpu as pltpu
from jax.sharding import PartitionSpec as P

EPSILON = 1e-06
MESH = pl.DeviceIdType.MESH
F32 = jnp.float32
BF16 = jnp.bfloat16


def body(
    resid_ref, gain_ref, unembed_hbm, targets_ref, ids_ref, decoder_hbm,
    out_ref,
    w_ref, dec_ref, nall, ebuf, dirbuf, rms_ref, gain_buf, uslab, gslab, idbuf,
    st_own, st_in, acc, crecv, sx, sy, rx, ry, s2x, s2y, r2x, r2y, zs, zr,
    bz, az, iz, bx, ax, ix,
    load_sem, gy_s, gy_r, gx_s, gx_r, gc_s, gc_r, gd_s, gd_r, st_s, st_r,
    c_s, c_r, x1_s, x1_r, y1_s, y1_r, x2_s, x2_r, y2_s, y2_r, z_s, z_r,
    bz_s, bz_r, az_s, az_r, iz_s, iz_r, fx_s, fx_r,
):
    tok = lax.axis_index("tok")
    voc = lax.axis_index("voc")
    x_lo = tok // 8
    y = (tok // 2) % 4
    core = tok % 2
    x_hi = voc // 8
    z = voc % 8
    x = x_hi * 2 + x_lo

    def device(xx, yy, zz, cc):
        return ((xx % 2) * 8 + yy * 2 + cc, (xx // 2) * 8 + zz)

    def x_peer(k):
        return device((x + k) % 4, y, z, core)

    def y_peer(k):
        return device(x, (y + k) % 4, z, core)

    def z_peer(k):
        return device(x, y, (z + k) % 8, core)

    sibling = device(x, y, z, 1 - core)

    def send(src, dst, s, r, peer):
        return pltpu.make_async_remote_copy(
            src_ref=src, dst_ref=dst, send_sem=s, recv_sem=r, device_id=peer, device_id_type=MESH
        )

    load_w = pltpu.make_async_copy(unembed_hbm, w_ref, load_sem.at[0])
    load_d = pltpu.make_async_copy(decoder_hbm, dec_ref, load_sem.at[1])
    load_w.start()
    load_d.start()
    barrier = pltpu.get_barrier_semaphore()
    peers = [sibling]
    peers += [x_peer(k) for k in (1, 2, 3)]
    peers += [y_peer(k) for k in (1, 2, 3)]
    peers += [z_peer(k) for k in range(1, 8)]
    for peer in peers:
        pl.semaphore_signal(barrier, inc=1, device_id=peer, device_id_type=MESH)

    hidden = resid_ref[...].astype(F32)
    width = hidden.shape[1]
    rms = jnp.sqrt(jnp.mean(hidden * hidden, axis=1, keepdims=True) + EPSILON)
    rms_ref[...] = jnp.broadcast_to(rms, rms_ref.shape)
    gain = gain_ref[...].reshape(1, width)
    gain_buf[...] = gain
    normed = (hidden / rms * gain).astype(BF16)
    for h in range(2):
        nall[h, x_lo, core, y] = normed[h * 16:h * 16 + 16]

    half = width // 2
    slab = half // 8
    start = pl.multiple_of(x_hi * half, half)
    unit_half = resid_ref[:, pl.ds(start, half)].astype(F32) / rms
    gain_half = gain_buf[:, pl.ds(start, half)]
    for zz in range(8):
        @pl.when(z == zz)
        def _():
            uslab[...] = unit_half[:, zz * slab:(zz + 1) * slab]
            gslab[...] = gain_half[:, zz * slab:(zz + 1) * slab]
    st_own[...] = jnp.zeros_like(st_own)
    idbuf[...] = jnp.zeros_like(idbuf)
    idbuf[:, 0:64] = ids_ref[...]

    pl.semaphore_wait(barrier, len(peers))

    def gy(h, k):
        part = nall.at[h, x_lo, core, y]
        return send(part, part, gy_s.at[h, k - 1], gy_r.at[h, k - 1], y_peer(k))

    def gx(h, kb):
        part = nall.at[h, x_lo, core, (y - kb + 4) % 4]
        return send(part, part, gx_s.at[h, kb], gx_r.at[h, kb], x_peer(1 if kb % 2 == 0 else 3))

    def gc(h, kb):
        part = nall.at[h, x_lo, core, (y - kb + 4) % 4]
        return send(part, part, gc_s.at[h, kb], gc_r.at[h, kb], sibling)

    def gd(h, kb):
        part = nall.at[h, 1 - x_lo, core, (y - kb + 4) % 4]
        return send(part, part, gd_s.at[h, kb], gd_r.at[h, kb], sibling)

    def pass_on(h, k):
        gy(h, k).wait_recv()
        gx(h, k).start()
        gc(h, k).start()

    def pass_over(h, kb):
        gx(h, kb).wait_recv()
        gd(h, kb).start()

    def gathered(h):
        for kb in (0, 1, 3, 2):
            gc(h, kb).wait_recv()
            gd(h, kb).wait_recv()

    for h in range(2):
        for k in (1, 3, 2):
            gy(h, k).start()
        gx(h, 0).start()
        gc(h, 0).start()

    low_half = lax.broadcasted_iota(jnp.int32, (16, 128), 1) < 64

    def attribute(values):
        high = values.astype(BF16)
        low = (values - high.astype(F32)).astype(BF16)
        stacked = jnp.concatenate([high, low], axis=0)
        lanes = jnp.bitwise_and(idbuf[...], 127)
        tiles = jnp.right_shift(idbuf[...], 7)

        def step(n, picked):
            cols = pl.ds(pl.multiple_of(n * 1024, 1024), 1024)
            both = jnp.dot(stacked, dec_ref[:, cols], preferred_element_type=F32)
            dots = both[0:32] + both[32:64]
            for q in range(8):
                got = jnp.take_along_axis(
                    dots[:, q * 128:(q + 1) * 128], lanes, axis=1, mode="promise_in_bounds"
                )
                picked = jnp.where(tiles == n * 8 + q, got, picked)
            return picked

        picked = lax.fori_loop(0, dec_ref.shape[1] // 1024, step, jnp.zeros((32, 128), F32))
        return jnp.where(low_half, picked[0:16], pltpu.roll(picked[16:32], 64, 1))

    def to_voc(buf, s, r):
        return [send(buf.at[z], buf.at[z], s.at[k - 1], r.at[k - 1], z_peer(k)) for k in range(1, 8)]

    load_d.wait()
    bz[z] = attribute(uslab[...])
    for copy in to_voc(bz, bz_s, bz_r):
        copy.start()

    eye = lax.broadcasted_iota(jnp.int32, (128, 128), 0) == lax.broadcasted_iota(jnp.int32, (128, 128), 1)

    def to_row(col):
        return jnp.sum(jnp.where(eye, col, 0.0), axis=0, keepdims=True)

    def to_col(row):
        return jnp.sum(jnp.where(eye, row, 0.0), axis=1, keepdims=True)

    def logits_of(h):
        def step(n, carry):
            cols = pl.ds(pl.multiple_of(n * 256, 256), 256)
            left = nall[h].reshape(256, width)
            ebuf[h, :, cols] = jnp.dot(left, w_ref[:, cols], preferred_element_type=F32)
            return carry

        lax.fori_loop(0, ebuf.shape[2] // 256, step, 0)
        for q in range(2):
            rows = pl.ds(q * 128, 128)
            part = ebuf[h, rows]
            top = jnp.max(part, axis=1, keepdims=True)
            part = jnp.exp(part - top)
            ebuf[h, rows] = part
            st_own[h, 0, pl.ds(q, 1)] = to_row(top)
            st_own[h, 0, pl.ds(2 + q, 1)] = to_row(jnp.sum(part, axis=1, keepdims=True))

    firsts = [0, 1, 4, 7, 14]

    def st_copies(h, stage):
        return [
            send(st_own.at[h, stage], st_in.at[h, n], st_s.at[h, n], st_r.at[h, n], peers[n])
            for n in range(firsts[stage], firsts[stage + 1])
        ]

    def st_send(h, stage):
        for copy in st_copies(h, stage):
            copy.start()

    def st_merge(h, stage):
        for copy in st_copies(h, stage):
            copy.wait_recv()
        tiles = [st_own[h, stage]] + [st_in[h, n] for n in range(firsts[stage], firsts[stage + 1])]
        merged = functools.reduce(jnp.maximum, [t[0:2] for t in tiles])
        st_own[h, stage + 1, 0:2] = merged
        st_own[h, stage + 1, 2:4] = sum(t[2:4] * jnp.exp(t[0:2] - merged) for t in tiles)
        if stage < 3:
            st_send(h, stage + 1)

    voc_cols = w_ref.shape[1]

    def direction_of(h):
        scale = jnp.exp(st_own[h, 0, 0:2] - st_own[h, 4, 0:2]) / st_own[h, 4, 2:4]
        lane = lax.broadcasted_iota(jnp.int32, (128, voc_cols), 1).astype(F32)
        rel = (targets_ref[...] - (tok * 16 + voc) * voc_cols).astype(F32)
        cols = [to_col(rel[n:n + 1]) for n in range(4)]
        for q in range(2):
            prob = ebuf[h, pl.ds(q * 128, 128)] * to_col(scale[q:q + 1])
            parts = []
            for cc in range(2):
                for yy in range(4):
                    first = (yy % 2) * 64 + cc * 32 + h * 16
                    parts.append(cols[q * 2 + yy // 2][first:first + 16])
            hot = jnp.where(lane == jnp.concatenate(parts, axis=0), 1.0, 0.0)
            dirbuf[h, pl.ds(q * 128, 128)] = (hot - prob).astype(BF16)

    for k in (1, 3, 2):
        pass_on(0, k)
    for k in (1, 3):
        pass_on(1, k)
    for kb in (0, 1, 3, 2):
        pass_over(0, kb)
    pass_on(1, 2)
    load_w.wait()
    gathered(0)
    logits_of(0)
    st_send(0, 0)
    for kb in (0, 1, 3):
        pass_over(1, kb)
    st_merge(0, 0)
    pass_over(1, 2)
    gathered(1)
    logits_of(1)
    st_send(1, 0)
    st_merge(0, 1)
    st_merge(1, 0)
    st_merge(0, 2)
    st_merge(1, 1)

    def cross(buf, n):
        return send(buf.at[0], buf.at[1], fx_s.at[n], fx_r.at[n], x_peer(2))

    def add_voc(buf, s, r, over, n):
        for copy in to_voc(buf, s, r):
            copy.wait_recv()
        over[0] = sum(buf[m] for m in range(8))
        cross(over, n).start()

    add_voc(bz, bz_s, bz_r, bx, 0)
    st_merge(0, 3)
    direction_of(0)

    def c_copy(j):
        return send(acc.at[1 - core, j], crecv.at[j], c_s.at[j], c_r.at[j], sibling)

    def x1(j, k):
        to = (x + k) % 4
        return send(sx.at[j, to // 2, to % 2], rx.at[j, k - 1], x1_s.at[j, k - 1], x1_r.at[j, k - 1], x_peer(k))

    def y1(j, k):
        return send(sy.at[j, (y + k) % 4], ry.at[j, k - 1], y1_s.at[j, k - 1], y1_r.at[j, k - 1], y_peer(k))

    def x2(j, k):
        to = (x + k) % 4
        return send(s2x.at[j, to // 2, to % 2], r2x.at[j, k - 1], x2_s.at[j, k - 1], x2_r.at[j, k - 1], x_peer(k))

    def y2(j, k):
        return send(s2y.at[j, (y + k) % 4], r2y.at[j, k - 1], y2_s.at[j, k - 1], y2_r.at[j, k - 1], y_peer(k))

    def z3(j, sub):
        hop = 2 * (j % 4) + sub
        slot = (j // 4, hop)
        return send(zs.at[j, sub], zr.at[slot], z_s.at[slot], z_r.at[slot], z_peer(hop + 1))

    def multiply(j):
        for sub in range(2):
            group = (z + 1 + 2 * (j % 4) + sub) % 8
            for hx in range(2):
                rows = pl.ds(pl.multiple_of(hx * half + group * slab, 32), slab)
                part = lax.dot_general(
                    dirbuf[j // 4], w_ref[rows, :], (((1,), (1,)), ((), ())), preferred_element_type=F32
                )
                for q in range(4):
                    acc[q % 2, j, hx, q // 2, :, sub] = part[q * 64:(q + 1) * 64].reshape(4, 16, slab)
        c_copy(j).start()

    def first_sum(j):
        c_copy(j).wait_recv()
        for hx in range(2):
            for xl in range(2):
                both = acc[core, j, hx, xl] + crecv[j, hx, xl]
                acc[core, j, hx, xl] = both
                sx[j, hx, xl] = both[:, :, 0:8].reshape(4, 16, slab).astype(BF16)
                for yy in range(4):
                    sy[j, yy, hx, xl] = both[yy, :, 8:16].reshape(16, slab).astype(BF16)
        for k in (2, 1, 3):
            x1(j, k).start()
            y1(j, k).start()

    def second_sum(j):
        for k in (1, 2, 3):
            x1(j, k).wait_recv()
        mine = acc[core, j, x_hi, x_lo, :, :, 0:8].reshape(4, 16, slab)
        for k in range(3):
            mine = mine + rx[j, k].astype(F32)
        acc[core, j, x_hi, x_lo, :, :, 0:8] = mine.reshape(4, 2, 8, slab)
        s2y[j] = mine.astype(BF16)
        for k in (2, 1, 3):
            y2(j, k).start()
        for k in (1, 2, 3):
            y1(j, k).wait_recv()
        other = acc[core, j, :, :, y, :, 8:16].reshape(2, 2, 16, slab)
        for k in range(3):
            other = other + ry[j, k].astype(F32)
        acc[core, j, :, :, y, :, 8:16] = other.reshape(2, 2, 2, 8, slab)
        s2x[j] = other.astype(BF16)
        for k in (2, 1, 3):
            x2(j, k).start()

    def third_sum(j):
        for k in (1, 2, 3):
            y2(j, k).wait_recv()
            x2(j, k).wait_recv()
        upper = acc[core, j, x_hi, x_lo, y, :, 0:8].reshape(16, slab)
        lower = acc[core, j, x_hi, x_lo, y, :, 8:16].reshape(16, slab)
        for k in range(3):
            upper = upper + r2y[j, k].astype(F32)
            lower = lower + r2x[j, k].astype(F32)
        for sub in range(2):
            zs[j, sub, 0:8] = upper[sub * 8:sub * 8 + 8]
            zs[j, sub, 8:16] = lower[sub * 8:sub * 8 + 8]
        z3(j, 0).start()

        @pl.when(j % 4 < 3)
        def _():
            z3(j, 1).start()

    def pipeline(i, carry):
        @pl.when(i == 1)
        def _():
            st_merge(1, 2)

        @pl.when(i == 4)
        def _():
            first_sum(i - 1)
            st_merge(1, 3)
            direction_of(1)

        @pl.when(i < 8)
        def _():
            multiply(i)

        @pl.when((i >= 1) & (i < 9) & (i != 4))
        def _():
            first_sum(i - 1)

        @pl.when((i >= 4) & (i < 12))
        def _():
            second_sum(i - 4)

        @pl.when(i >= 6)
        def _():
            third_sum(i - 6)

        return carry

    lax.fori_loop(0, 14, pipeline, 0)
    grads = []
    for h in range(2):
        total = zs[h * 4 + 3, 1]
        for hop in range(7):
            z3(h * 4 + hop // 2, hop % 2).wait_recv()
            total = total + zr[h, hop]
        grads.append(total)
    grad = jnp.concatenate(grads, axis=0)

    scaled = grad * gslab[...]
    inner = jnp.sum(uslab[...] * scaled, axis=1, keepdims=True)
    iz[z] = jnp.broadcast_to(inner, (32, 128))
    for copy in to_voc(iz, iz_s, iz_r):
        copy.start()
    az[z] = attribute(scaled)
    for copy in to_voc(az, az_s, az_r):
        copy.start()
    add_voc(iz, iz_s, iz_r, ix, 1)
    add_voc(az, az_s, az_r, ax, 2)
    cross(bx, 0).wait_recv()
    cross(ix, 1).wait_recv()
    unit_dot = bx[0] + bx[1]
    mean = (ix[0] + ix[1]) * (1.0 / width)
    scale = 1.0 / rms_ref[...]
    cross(ax, 2).wait_recv()
    both = ax[0] + ax[1]
    for n in range(2):
        rows = slice(n * 16, n * 16 + 16)
        if n == 1:
            both = pltpu.roll(both, 64, 1)
            unit_dot = pltpu.roll(unit_dot, 64, 1)
        out_ref[rows] = ((both - unit_dot * mean[rows]) * scale[rows])[:, 0:64]

    for h in range(2):
        for k in (1, 2, 3):
            gy(h, k).wait_send()
        for kb in range(4):
            gx(h, kb).wait_send()
            gc(h, kb).wait_send()
            gd(h, kb).wait_send()
        for stage in range(4):
            for copy in st_copies(h, stage):
                copy.wait_send()

    def drain(j, carry):
        c_copy(j).wait_send()
        for k in (1, 2, 3):
            x1(j, k).wait_send()
            y1(j, k).wait_send()
            x2(j, k).wait_send()
            y2(j, k).wait_send()

        z3(j, 0).wait_send()

        @pl.when(j % 4 < 3)
        def _():
            z3(j, 1).wait_send()

        return carry

    lax.fori_loop(0, 8, drain, 0)
    for copy in to_voc(bz, bz_s, bz_r) + to_voc(az, az_s, az_r) + to_voc(iz, iz_s, iz_r):
        copy.wait_send()
    for n, over in enumerate((bx, ix, ax)):
        cross(over, n).wait_send()


def on_device(resid, norm_gain, unembed, targets, feat_ids, feat_acts, decoder):
    width = resid.shape[1]
    voc_cols = unembed.shape[1]
    slab, features = decoder.shape
    vm = pl.BlockSpec(memory_space=pltpu.VMEM)
    hbm = pl.BlockSpec(memory_space=pl.ANY)
    dma = pltpu.SemaphoreType.DMA
    projected = pl.pallas_call(
        body,
        out_shape=jax.ShapeDtypeStruct(feat_acts.shape, F32),
        in_specs=[vm, vm, hbm, vm, vm, hbm],
        out_specs=vm,
        scratch_shapes=[
            pltpu.VMEM(unembed.shape, BF16),
            pltpu.VMEM(decoder.shape, BF16),
            pltpu.VMEM((2, 2, 2, 4, 16, width), BF16),
            pltpu.VMEM((2, 256, voc_cols), F32),
            pltpu.VMEM((2, 256, voc_cols), BF16),
            pltpu.VMEM((32, 128), F32),
            pltpu.VMEM((1, width), F32),
            pltpu.VMEM((32, slab), F32),
            pltpu.VMEM((1, slab), F32),
            pltpu.VMEM((32, 128), jnp.int32),
            pltpu.VMEM((2, 5, 8, 128), F32),
            pltpu.VMEM((2, 14, 8, 128), F32),
            pltpu.VMEM((2, 8, 2, 2, 4, 2, 16, slab), F32),
            pltpu.VMEM((8, 2, 2, 4, 2, 16, slab), F32),
            pltpu.VMEM((8, 2, 2, 4, 16, slab), BF16),
            pltpu.VMEM((8, 4, 2, 2, 16, slab), BF16),
            pltpu.VMEM((8, 3, 4, 16, slab), BF16),
            pltpu.VMEM((8, 3, 2, 2, 16, slab), BF16),
            pltpu.VMEM((8, 2, 2, 16, slab), BF16),
            pltpu.VMEM((8, 4, 16, slab), BF16),
            pltpu.VMEM((8, 3, 16, slab), BF16),
            pltpu.VMEM((8, 3, 16, slab), BF16),
            pltpu.VMEM((8, 2, 16, slab), F32),
            pltpu.VMEM((2, 7, 16, slab), F32),
            pltpu.VMEM((8, 16, 128), F32),
            pltpu.VMEM((8, 16, 128), F32),
            pltpu.VMEM((8, 32, 128), F32),
            pltpu.VMEM((2, 16, 128), F32),
            pltpu.VMEM((2, 16, 128), F32),
            pltpu.VMEM((2, 32, 128), F32),
            dma((2,)),
            dma((2, 3)), dma((2, 3)),
            dma((2, 4)), dma((2, 4)),
            dma((2, 4)), dma((2, 4)),
            dma((2, 4)), dma((2, 4)),
            dma((2, 14)), dma((2, 14)),
            dma((8,)), dma((8,)),
            dma((8, 3)), dma((8, 3)),
            dma((8, 3)), dma((8, 3)),
            dma((8, 3)), dma((8, 3)),
            dma((8, 3)), dma((8, 3)),
            dma((2, 7)), dma((2, 7)),
            dma((7,)), dma((7,)),
            dma((7,)), dma((7,)),
            dma((7,)), dma((7,)),
            dma((3,)), dma((3,)),
        ],
        compiler_params=pltpu.CompilerParams(
            collective_id=0, has_side_effects=True, vmem_limit_bytes=60 * 1024 * 1024
        ),
    )(resid, norm_gain, unembed, targets.reshape(4, 128), feat_ids, decoder)
    return projected * feat_acts


def solution(mesh):
    placed = (
        P("tok", None),
        P(),
        P(None, ("tok", "voc")),
        P(),
        P("tok", None),
        P("tok", None),
        P("voc", None),
    )
    return jax.shard_map(
        on_device, mesh=mesh, in_specs=placed, out_specs=P("tok", None), check_vma=False
    )
```

time: 85.6 us -> 84.5 us (0.987)
  no operation moved by 1% of the time
where the time goes in v3:
time: 84.5 us; the launch traced here: 84.2 us
  Pallas kernels  82.8 us (98%)
  other arithmetic  1.33 us (2%)
    pallas_call x1, Pallas kernels, on_device(): pl.pallas_call(body, out_shape=jax.ShapeDtypeStruct(feat_acts.shape, F32)...  82.8 us

profile of v3, /device:TPU:32, one launch (start us, length us, event | category | flops | bytes accessed | tf_op | source)
XLA Modules:
  0.0 84.2 jit_solution(2390924553428703989)
XLA Ops:
  0.0 0.0 copy-start
  0.0 82.8 %shard_map.73 = f32[32,64]{1,0:T(8,128)} custom-call(bf16[32,3584]{1,0:T(8,128)(2,1)} %resid_ref.1, f32[3584]{0:T(1024)} %gain_ref.1, bf16[3584,768]{1,0:T(8,128)(2,1)} %unembed_hbm.1, s32[4,128]{1,0:T(4,128)} %bitcast.1, s32[32,64]{1,0:T(8,128)} %ids_ref.1, bf16[224,16384]{1,0:T(8,128)(2,1)} %decoder_hbm.1), custom_call_target="tpu_custom_call" | custom-call | tf_op jit(solution)/shard_map/pallas_call | solution.py:448
  82.8 0.0 copy-done
  82.8 1.3 %mul.3 = f32[32,64]{1,0:T(8,128)} multiply(f32[32,64]{1,0:T(8,128)} %shard_map.73, f32[32,64]{1,0:T(8,128)S(1)} %copy-done) | non-fusion elementwise | flops 2048 | bytes 24576 | tf_op jit(solution)/shard_map/mul | solution.py:505
Async XLA Ops:
  0.0 82.8 %copy-start = (f32[32,64]{1,0:T(8,128)S(1)}, f32[32,64]{1,0:T(8,128)}, u32[]{:S(2)}) copy-start(f32[32,64]{1,0:T(8,128)} %param.12) | copy-start | bytes 24580

commit v4 on v3

--- a/solution.py
+++ b/solution.py
@@ -11,6 +11,9 @@
 MESH = pl.DeviceIdType.MESH
 F32 = jnp.float32
 BF16 = jnp.bfloat16
+CHUNK = 2048
+LAG2 = 4
+LAG3 = 6
 
 
 def body(
@@ -60,6 +63,10 @@
     peers += [x_peer(k) for k in (1, 2, 3)]
     peers += [y_peer(k) for k in (1, 2, 3)]
     peers += [z_peer(k) for k in range(1, 8)]
+    plane = [(a, b) for a in range(4) for b in range(4) if a + b > 0]
+    crossed = [device((x + a) % 4, (y + b) % 4, z, core) for a, b in plane]
+    stat_peers = peers[0:1] + crossed + peers[7:14]
+    peers = stat_peers
     for peer in peers:
         pl.semaphore_signal(barrier, inc=1, device_id=peer, device_id_type=MESH)
 
@@ -75,6 +82,47 @@
 
     half = width // 2
     slab = half // 8
+    pl.semaphore_wait(barrier, len(peers))
+
+    def gy(h, k):
+        part = nall.at[h, x_lo, core, y]
+        return send(part, part, gy_s.at[h, k - 1], gy_r.at[h, k - 1], y_peer(k))
+
+    def gx(h, kb, d):
+        part = nall.at[h, x_lo, core, (y - kb + 4) % 4, :, pl.ds(d * half, half)]
+        return send(part, part, gx_s.at[h, kb, d], gx_r.at[h, kb, d], x_peer(1 + 2 * d))
+
+    def gc(h, kb):
+        part = nall.at[h, x_lo, core, (y - kb + 4) % 4]
+        return send(part, part, gc_s.at[h, kb], gc_r.at[h, kb], sibling)
+
+    def gd(h, kb):
+        part = nall.at[h, 1 - x_lo, core, (y - kb + 4) % 4]
+        return send(part, part, gd_s.at[h, kb], gd_r.at[h, kb], sibling)
+
+    def pass_on(h, k):
+        gy(h, k).wait_recv()
+        gx(h, k, 0).start()
+        gx(h, k, 1).start()
+        gc(h, k).start()
+
+    def pass_over(h, kb):
+        gx(h, kb, 0).wait_recv()
+        gx(h, kb, 1).wait_recv()
+        gd(h, kb).start()
+
+    def gathered(h, own):
+        for kb in (0, 1, 3, 2):
+            (gc if own else gd)(h, kb).wait_recv()
+
+    for k in (1, 3, 2):
+        gy(0, k).start()
+    for h in range(2):
+        gx(h, 0, 0).start()
+        gx(h, 0, 1).start()
+    gc(0, 0).start()
+    gc(1, 0).start()
+
     start = pl.multiple_of(x_hi * half, half)
     unit_half = resid_ref[:, pl.ds(start, half)].astype(F32) / rms
     gain_half = gain_buf[:, pl.ds(start, half)]
@@ -86,45 +134,6 @@
     st_own[...] = jnp.zeros_like(st_own)
     idbuf[...] = jnp.zeros_like(idbuf)
     idbuf[:, 0:64] = ids_ref[...]
-
-    pl.semaphore_wait(barrier, len(peers))
-
-    def gy(h, k):
-        part = nall.at[h, x_lo, core, y]
-        return send(part, part, gy_s.at[h, k - 1], gy_r.at[h, k - 1], y_peer(k))
-
-    def gx(h, kb):
-        part = nall.at[h, x_lo, core, (y - kb + 4) % 4]
-        return send(part, part, gx_s.at[h, kb], gx_r.at[h, kb], x_peer(1 if kb % 2 == 0 else 3))
-
-    def gc(h, kb):
-        part = nall.at[h, x_lo, core, (y - kb + 4) % 4]
-        return send(part, part, gc_s.at[h, kb], gc_r.at[h, kb], sibling)
-
-    def gd(h, kb):
-        part = nall.at[h, 1 - x_lo, core, (y - kb + 4) % 4]
-        return send(part, part, gd_s.at[h, kb], gd_r.at[h, kb], sibling)
-
-    def pass_on(h, k):
-        gy(h, k).wait_recv()
-        gx(h, k).start()
-        gc(h, k).start()
-
-    def pass_over(h, kb):
-        gx(h, kb).wait_recv()
-        gd(h, kb).start()
-
-    def gathered(h):
-        for kb in (0, 1, 3, 2):
-            gc(h, kb).wait_recv()
-            gd(h, kb).wait_recv()
-
-    for h in range(2):
-        for k in (1, 3, 2):
-            gy(h, k).start()
-        gx(h, 0).start()
-        gc(h, 0).start()
-
     low_half = lax.broadcasted_iota(jnp.int32, (16, 128), 1) < 64
 
     def attribute(values):
@@ -135,17 +144,17 @@
         tiles = jnp.right_shift(idbuf[...], 7)
 
         def step(n, picked):
-            cols = pl.ds(pl.multiple_of(n * 1024, 1024), 1024)
+            cols = pl.ds(pl.multiple_of(n * CHUNK, CHUNK), CHUNK)
             both = jnp.dot(stacked, dec_ref[:, cols], preferred_element_type=F32)
             dots = both[0:32] + both[32:64]
-            for q in range(8):
+            for q in range(CHUNK // 128):
                 got = jnp.take_along_axis(
                     dots[:, q * 128:(q + 1) * 128], lanes, axis=1, mode="promise_in_bounds"
                 )
-                picked = jnp.where(tiles == n * 8 + q, got, picked)
+                picked = jnp.where(tiles == n * (CHUNK // 128) + q, got, picked)
             return picked
 
-        picked = lax.fori_loop(0, dec_ref.shape[1] // 1024, step, jnp.zeros((32, 128), F32))
+        picked = lax.fori_loop(0, dec_ref.shape[1] // CHUNK, step, jnp.zeros((32, 128), F32))
         return jnp.where(low_half, picked[0:16], pltpu.roll(picked[16:32], 64, 1))
 
     def to_voc(buf, s, r):
@@ -164,28 +173,28 @@
     def to_col(row):
         return jnp.sum(jnp.where(eye, row, 0.0), axis=1, keepdims=True)
 
-    def logits_of(h):
+    def logits_of(h, xl):
+        rows = pl.ds(pl.multiple_of(xl * 128, 128), 128)
+        left = nall[h, xl].reshape(128, width)
+
         def step(n, carry):
             cols = pl.ds(pl.multiple_of(n * 256, 256), 256)
-            left = nall[h].reshape(256, width)
-            ebuf[h, :, cols] = jnp.dot(left, w_ref[:, cols], preferred_element_type=F32)
+            ebuf[h, rows, cols] = jnp.dot(left, w_ref[:, cols], preferred_element_type=F32)
             return carry
 
         lax.fori_loop(0, ebuf.shape[2] // 256, step, 0)
-        for q in range(2):
-            rows = pl.ds(q * 128, 128)
-            part = ebuf[h, rows]
-            top = jnp.max(part, axis=1, keepdims=True)
-            part = jnp.exp(part - top)
-            ebuf[h, rows] = part
-            st_own[h, 0, pl.ds(q, 1)] = to_row(top)
-            st_own[h, 0, pl.ds(2 + q, 1)] = to_row(jnp.sum(part, axis=1, keepdims=True))
-
-    firsts = [0, 1, 4, 7, 14]
+        part = ebuf[h, rows]
+        top = jnp.max(part, axis=1, keepdims=True)
+        part = jnp.exp(part - top)
+        ebuf[h, rows] = part
+        st_own[h, 0, pl.ds(xl, 1)] = to_row(top)
+        st_own[h, 0, pl.ds(2 + xl, 1)] = to_row(jnp.sum(part, axis=1, keepdims=True))
+
+    firsts = [0, 1, 16, 23]
 
     def st_copies(h, stage):
         return [
-            send(st_own.at[h, stage], st_in.at[h, n], st_s.at[h, n], st_r.at[h, n], peers[n])
+            send(st_own.at[h, stage], st_in.at[h, n], st_s.at[h, n], st_r.at[h, n], stat_peers[n])
             for n in range(firsts[stage], firsts[stage + 1])
         ]
 
@@ -200,13 +209,13 @@
         merged = functools.reduce(jnp.maximum, [t[0:2] for t in tiles])
         st_own[h, stage + 1, 0:2] = merged
         st_own[h, stage + 1, 2:4] = sum(t[2:4] * jnp.exp(t[0:2] - merged) for t in tiles)
-        if stage < 3:
+        if stage < 2:
             st_send(h, stage + 1)
 
     voc_cols = w_ref.shape[1]
 
     def direction_of(h):
-        scale = jnp.exp(st_own[h, 0, 0:2] - st_own[h, 4, 0:2]) / st_own[h, 4, 2:4]
+        scale = jnp.exp(st_own[h, 0, 0:2] - st_own[h, 3, 0:2]) / st_own[h, 3, 2:4]
         lane = lax.broadcasted_iota(jnp.int32, (128, voc_cols), 1).astype(F32)
         rel = (targets_ref[...] - (tok * 16 + voc) * voc_cols).astype(F32)
         cols = [to_col(rel[n:n + 1]) for n in range(4)]
@@ -221,27 +230,35 @@
             dirbuf[h, pl.ds(q * 128, 128)] = (hot - prob).astype(BF16)
 
     for k in (1, 3, 2):
-        pass_on(0, k)
-    for k in (1, 3):
-        pass_on(1, k)
-    for kb in (0, 1, 3, 2):
-        pass_over(0, kb)
+        gy(1, k).start()
+    pass_on(0, 1)
+    pass_on(0, 3)
+    pass_over(0, 0)
+    pass_on(0, 2)
+    pass_over(1, 0)
+    pass_over(0, 1)
+    pass_over(0, 3)
+    pass_on(1, 1)
+    pass_on(1, 3)
+    pass_over(0, 2)
     pass_on(1, 2)
     load_w.wait()
-    gathered(0)
-    logits_of(0)
+    gathered(0, True)
+    logits_of(0, x_lo)
+    gathered(0, False)
+    logits_of(0, 1 - x_lo)
     st_send(0, 0)
-    for kb in (0, 1, 3):
-        pass_over(1, kb)
+    pass_over(1, 1)
+    pass_over(1, 3)
     st_merge(0, 0)
     pass_over(1, 2)
-    gathered(1)
-    logits_of(1)
+    gathered(1, True)
+    logits_of(1, x_lo)
+    gathered(1, False)
+    logits_of(1, 1 - x_lo)
     st_send(1, 0)
+    st_merge(1, 0)
     st_merge(0, 1)
-    st_merge(1, 0)
-    st_merge(0, 2)
-    st_merge(1, 1)
 
     def cross(buf, n):
         return send(buf.at[0], buf.at[1], fx_s.at[n], fx_r.at[n], x_peer(2))
@@ -253,7 +270,7 @@
         cross(over, n).start()
 
     add_voc(bz, bz_s, bz_r, bx, 0)
-    st_merge(0, 3)
+    st_merge(0, 2)
     direction_of(0)
 
     def c_copy(j):
@@ -344,33 +361,33 @@
     def pipeline(i, carry):
         @pl.when(i == 1)
         def _():
+            st_merge(1, 1)
+
+        @pl.when(i == 4)
+        def _():
+            first_sum(i - 1)
             st_merge(1, 2)
-
-        @pl.when(i == 4)
+            direction_of(1)
+
+        @pl.when(i < 8)
+        def _():
+            multiply(i)
+
+        @pl.when((i >= 1) & (i < 9) & (i != 4))
         def _():
             first_sum(i - 1)
-            st_merge(1, 3)
-            direction_of(1)
-
-        @pl.when(i < 8)
-        def _():
-            multiply(i)
-
-        @pl.when((i >= 1) & (i < 9) & (i != 4))
-        def _():
-            first_sum(i - 1)
-
-        @pl.when((i >= 4) & (i < 12))
-        def _():
-            second_sum(i - 4)
-
-        @pl.when(i >= 6)
-        def _():
-            third_sum(i - 6)
+
+        @pl.when((i >= LAG2) & (i < 8 + LAG2))
+        def _():
+            second_sum(i - LAG2)
+
+        @pl.when(i >= LAG3)
+        def _():
+            third_sum(i - LAG3)
 
         return carry
 
-    lax.fori_loop(0, 14, pipeline, 0)
+    lax.fori_loop(0, 8 + LAG3, pipeline, 0)
     grads = []
     for h in range(2):
         total = zs[h * 4 + 3, 1]
@@ -389,6 +406,35 @@
     for copy in to_voc(az, az_s, az_r):
         copy.start()
     add_voc(iz, iz_s, iz_r, ix, 1)
+    for h in range(2):
+        for k in (1, 2, 3):
+            gy(h, k).wait_send()
+        for kb in range(4):
+            gx(h, kb, 0).wait_send()
+            gx(h, kb, 1).wait_send()
+            gc(h, kb).wait_send()
+            gd(h, kb).wait_send()
+        for stage in range(3):
+            for copy in st_copies(h, stage):
+                copy.wait_send()
+
+    def drain(j, carry):
+        c_copy(j).wait_send()
+        for k in (1, 2, 3):
+            x1(j, k).wait_send()
+            y1(j, k).wait_send()
+            x2(j, k).wait_send()
+            y2(j, k).wait_send()
+
+        z3(j, 0).wait_send()
+
+        @pl.when(j % 4 < 3)
+        def _():
+            z3(j, 1).wait_send()
+
+        return carry
+
+    lax.fori_loop(0, 8, drain, 0)
     add_voc(az, az_s, az_r, ax, 2)
     cross(bx, 0).wait_recv()
     cross(ix, 1).wait_recv()
@@ -404,34 +450,6 @@
             unit_dot = pltpu.roll(unit_dot, 64, 1)
         out_ref[rows] = ((both - unit_dot * mean[rows]) * scale[rows])[:, 0:64]
 
-    for h in range(2):
-        for k in (1, 2, 3):
-            gy(h, k).wait_send()
-        for kb in range(4):
-            gx(h, kb).wait_send()
-            gc(h, kb).wait_send()
-            gd(h, kb).wait_send()
-        for stage in range(4):
-            for copy in st_copies(h, stage):
-                copy.wait_send()
-
-    def drain(j, carry):
-        c_copy(j).wait_send()
-        for k in (1, 2, 3):
-            x1(j, k).wait_send()
-            y1(j, k).wait_send()
-            x2(j, k).wait_send()
-            y2(j, k).wait_send()
-
-        z3(j, 0).wait_send()
-
-        @pl.when(j % 4 < 3)
-        def _():
-            z3(j, 1).wait_send()
-
-        return carry
-
-    lax.fori_loop(0, 8, drain, 0)
     for copy in to_voc(bz, bz_s, bz_r) + to_voc(az, az_s, az_r) + to_voc(iz, iz_s, iz_r):
         copy.wait_send()
     for n, over in enumerate((bx, ix, ax)):
@@ -461,8 +479,8 @@
             pltpu.VMEM((32, slab), F32),
             pltpu.VMEM((1, slab), F32),
             pltpu.VMEM((32, 128), jnp.int32),
-            pltpu.VMEM((2, 5, 8, 128), F32),
-            pltpu.VMEM((2, 14, 8, 128), F32),
+            pltpu.VMEM((2, 4, 8, 128), F32),
+            pltpu.VMEM((2, 23, 8, 128), F32),
             pltpu.VMEM((2, 8, 2, 2, 4, 2, 16, slab), F32),
             pltpu.VMEM((8, 2, 2, 4, 2, 16, slab), F32),
             pltpu.VMEM((8, 2, 2, 4, 16, slab), BF16),
@@ -483,10 +501,10 @@
             pltpu.VMEM((2, 32, 128), F32),
             dma((2,)),
             dma((2, 3)), dma((2, 3)),
+            dma((2, 4, 2)), dma((2, 4, 2)),
             dma((2, 4)), dma((2, 4)),
             dma((2, 4)), dma((2, 4)),
-            dma((2, 4)), dma((2, 4)),
-            dma((2, 14)), dma((2, 14)),
+            dma((2, 23)), dma((2, 23)),
             dma((8,)), dma((8,)),
             dma((8, 3)), dma((8, 3)),
             dma((8, 3)), dma((8, 3)),

time: 84.5 us -> 77.8 us (0.921)
  Pallas kernels: 82.8 us -> 76 us
    pallas_call x1, Pallas kernels: 82.8 us -> 76 us  [on_device(): pl.pallas_call(body, out_shape=jax.ShapeDtypeStruct(feat_acts.shape, F32)...]
where the time goes in v4:
time: 77.8 us; the launch traced here: 77.4 us
  Pallas kernels  76 us (98%)
  other arithmetic  1.33 us (2%)
    pallas_call x1, Pallas kernels, on_device(): pl.pallas_call(body, out_shape=jax.ShapeDtypeStruct(feat_acts.shape, F32)...  76 us

profile of v4, /device:TPU:32, one launch (start us, length us, event | category | flops | bytes accessed | tf_op | source)
XLA Modules:
  0.0 77.4 jit_solution(3825664550390704575)
XLA Ops:
  0.0 0.0 copy-start
  0.0 76.0 %shard_map.73 = f32[32,64]{1,0:T(8,128)} custom-call(bf16[32,3584]{1,0:T(8,128)(2,1)} %resid_ref.1, f32[3584]{0:T(1024)} %gain_ref.1, bf16[3584,768]{1,0:T(8,128)(2,1)} %unembed_hbm.1, s32[4,128]{1,0:T(4,128)} %bitcast.1, s32[32,64]{1,0:T(8,128)} %ids_ref.1, bf16[224,16384]{1,0:T(8,128)(2,1)} %decoder_hbm.1), custom_call_target="tpu_custom_call" | custom-call | tf_op jit(solution)/shard_map/pallas_call | solution.py:466
  76.0 0.0 copy-done
  76.0 1.3 %mul.3 = f32[32,64]{1,0:T(8,128)} multiply(f32[32,64]{1,0:T(8,128)} %shard_map.73, f32[32,64]{1,0:T(8,128)S(1)} %copy-done) | non-fusion elementwise | flops 2048 | bytes 24576 | tf_op jit(solution)/shard_map/mul | solution.py:523
Async XLA Ops:
  0.0 76.0 %copy-start = (f32[32,64]{1,0:T(8,128)S(1)}, f32[32,64]{1,0:T(8,128)}, u32[]{:S(2)}) copy-start(f32[32,64]{1,0:T(8,128)} %param.12) | copy-start | bytes 24580

commit v5 on v4

--- a/solution.py
+++ b/solution.py
@@ -11,7 +11,7 @@
 MESH = pl.DeviceIdType.MESH
 F32 = jnp.float32
 BF16 = jnp.bfloat16
-CHUNK = 2048
+CHUNK = 8192
 LAG2 = 4
 LAG3 = 6
 

time: 77.8 us -> 76.9 us (0.988)
  no operation moved by 1% of the time
where the time goes in v5:
time: 76.9 us; the launch traced here: 76.7 us
  Pallas kernels  75.4 us (98%)
  other arithmetic  1.33 us (2%)
    pallas_call x1, Pallas kernels, on_device(): pl.pallas_call(body, out_shape=jax.ShapeDtypeStruct(feat_acts.shape, F32)...  75.4 us

profile of v5, /device:TPU:32, one launch (start us, length us, event | category | flops | bytes accessed | tf_op | source)
XLA Modules:
  0.0 76.7 jit_solution(11345259271132034120)
XLA Ops:
  0.0 0.0 copy-start
  0.0 75.4 %shard_map.73 = f32[32,64]{1,0:T(8,128)} custom-call(bf16[32,3584]{1,0:T(8,128)(2,1)} %resid_ref.1, f32[3584]{0:T(1024)} %gain_ref.1, bf16[3584,768]{1,0:T(8,128)(2,1)} %unembed_hbm.1, s32[4,128]{1,0:T(4,128)} %bitcast.1, s32[32,64]{1,0:T(8,128)} %ids_ref.1, bf16[224,16384]{1,0:T(8,128)(2,1)} %decoder_hbm.1), custom_call_target="tpu_custom_call" | custom-call | tf_op jit(solution)/shard_map/pallas_call | solution.py:466
  75.4 0.0 copy-done
  75.4 1.3 %mul.3 = f32[32,64]{1,0:T(8,128)} multiply(f32[32,64]{1,0:T(8,128)} %shard_map.73, f32[32,64]{1,0:T(8,128)S(1)} %copy-done) | non-fusion elementwise | flops 2048 | bytes 24576 | tf_op jit(solution)/shard_map/mul | solution.py:523
Async XLA Ops:
  0.0 75.4 %copy-start = (f32[32,64]{1,0:T(8,128)S(1)}, f32[32,64]{1,0:T(8,128)}, u32[]{:S(2)}) copy-start(f32[32,64]{1,0:T(8,128)} %param.12) | copy-start | bytes 24580

commit v6 on v5

--- a/solution.py
+++ b/solution.py
@@ -11,7 +11,7 @@
 MESH = pl.DeviceIdType.MESH
 F32 = jnp.float32
 BF16 = jnp.bfloat16
-CHUNK = 8192
+CHUNK = 16384
 LAG2 = 4
 LAG3 = 6
 

time: 76.9 us -> 77.3 us (level)
  no operation moved by 1% of the time
where the time goes in v6:
time: 77.3 us; the launch traced here: 77.1 us
  Pallas kernels  75.7 us (98%)
  other arithmetic  1.33 us (2%)
    pallas_call x1, Pallas kernels, on_device(): pl.pallas_call(body, out_shape=jax.ShapeDtypeStruct(feat_acts.shape, F32)...  75.7 us

profile of v6, /device:TPU:32, one launch (start us, length us, event | category | flops | bytes accessed | tf_op | source)
XLA Modules:
  0.0 77.1 jit_solution(15863607222186324178)
XLA Ops:
  0.0 0.0 copy-start
  0.0 75.7 %shard_map.73 = f32[32,64]{1,0:T(8,128)} custom-call(bf16[32,3584]{1,0:T(8,128)(2,1)} %resid_ref.1, f32[3584]{0:T(1024)} %gain_ref.1, bf16[3584,768]{1,0:T(8,128)(2,1)} %unembed_hbm.1, s32[4,128]{1,0:T(4,128)} %bitcast.1, s32[32,64]{1,0:T(8,128)} %ids_ref.1, bf16[224,16384]{1,0:T(8,128)(2,1)} %decoder_hbm.1), custom_call_target="tpu_custom_call" | custom-call | tf_op jit(solution)/shard_map/pallas_call | solution.py:466
  75.7 0.0 copy-done
  75.7 1.3 %mul.3 = f32[32,64]{1,0:T(8,128)} multiply(f32[32,64]{1,0:T(8,128)} %shard_map.73, f32[32,64]{1,0:T(8,128)S(1)} %copy-done) | non-fusion elementwise | flops 2048 | bytes 24576 | tf_op jit(solution)/shard_map/mul | solution.py:523
Async XLA Ops:
  0.0 75.7 %copy-start = (f32[32,64]{1,0:T(8,128)S(1)}, f32[32,64]{1,0:T(8,128)}, u32[]{:S(2)}) copy-start(f32[32,64]{1,0:T(8,128)} %param.12) | copy-start | bytes 24580
